TPU v7x, 512 devices: a whole 4x4x16 slice. The times are simulated.
512 devices in a mesh: ctx: 128 (over x, z, core), head: 4 (over y).
Axes of the slice: x: 4, y: 4, z: 16, core: 2. Of those that a mesh axis runs over, the one named last changes fastest.
Arguments:
- queries: bfloat16 [16, 32768, 128], P('head', 'ctx'), may hold values from -6 to 6
- key_vectors: bfloat16 [16, 32768, 128], P('head', 'ctx'), may hold values from -6 to 6
- value_vectors: bfloat16 [16, 32768, 128], P('head', 'ctx'), may hold values from -12 to 12
- norm_gain: float32 [16, 128], P('head'), may hold values from 0.5 to 1.5
- upstream: bfloat16 [16, 32768, 128], P('head', 'ctx'), may hold values from -6 to 6
- cluster_ids: int32 [16, 32768, 1], P('head', 'ctx'), may hold values from 0 to 255; in each aligned block of 256 rows (0 to 255, 256 to 511, ..., all dimensions but the last counted through in order) at most 2 rows name the same one
- positions: int32 [32768], P('ctx'), may hold values from 0 to 32767, each once
Outputs:
- normed_out: bfloat16 [16, 32768, 128], P('head', 'ctx')
- grad_queries: bfloat16 [16, 32768, 128], P('head', 'ctx')
- grad_keys: bfloat16 [16, 32768, 128], P('head', 'ctx')
- grad_values: bfloat16 [16, 32768, 128], P('head', 'ctx')
- centroids: float32 [256, 16, 128], P('ctx', 'head')
Inputs may be any that keep to these rules, and one draw needn't show every extreme that they name: `cluster_ids`: within one head, the 256 tokens of one index of ctx name one cluster at most 2 times. `positions`: every position appears once.
All inputs are finite; a program needn't handle non-finite values.
Results may differ from a plain program's by a relative error of at most 0.02.
Values may be sent and summed in bfloat16 or wider, within the bound.
No kernel may reach another device: no remote copies, remote signals or barrier semaphores. Data moves between devices by JAX's collectives and lax.ppermute only.
A program may use at most 64 MiB of HBM per device.

v0:
```python
import jax
import jax.numpy as jnp
from jax import lax
from jax.sharding import PartitionSpec as P

CLUSTERS = 256
SEND_CAP = 2


def rank_within(member):
    tok_count = member.shape[1]
    matches = member[:, :, None] == member[:, None, :]
    earlier = lax.broadcasted_iota(jnp.int32, (tok_count, tok_count), 0) > lax.broadcasted_iota(
        jnp.int32, (tok_count, tok_count), 1
    )
    return jnp.sum(jnp.logical_and(matches, earlier[None]), axis=2, dtype=jnp.int32)


def weights_of(query_block, key_block, slot_pos, factor):
    scores = (
        jnp.einsum("urd,ujd->urj", query_block, key_block, preferred_element_type=jnp.float32)
        * factor
    )
    allowed = jnp.logical_and(
        slot_pos[:, None, :] >= 0, slot_pos[:, None, :] <= slot_pos[:, :, None]
    )
    scores = jnp.where(allowed, scores, -1e30)
    highest = jnp.max(scores, axis=2, keepdims=True)
    exponent = jnp.exp(scores - highest)
    return exponent / jnp.sum(exponent, axis=2, keepdims=True)


def local(queries, key_vectors, value_vectors, norm_gain, upstream, cluster_ids, positions):
    heads, tokens, feature = queries.shape
    n_ctx = lax.axis_size("ctx")
    per_dev = CLUSTERS // n_ctx
    factor = feature ** (-0.5)
    member = cluster_ids[:, :, 0]
    target = member * SEND_CAP + rank_within(member)
    slots = CLUSTERS * SEND_CAP
    mine = slots // n_ctx
    onehot = target[:, None, :] == lax.broadcasted_iota(jnp.int32, (1, slots, 1), 1)
    place = onehot.astype(jnp.bfloat16)

    def to_owner(source):
        placed = jnp.einsum(
            "hst,htd->hsd", place, source, preferred_element_type=jnp.float32
        ).astype(jnp.bfloat16)
        placed = placed.reshape(heads, n_ctx, mine, source.shape[2])
        placed = placed.transpose(1, 0, 2, 3).reshape(n_ctx, heads * mine, source.shape[2])
        return lax.all_to_all(placed, "ctx", 0, 0, tiled=True)

    def from_owner(block):
        back = lax.all_to_all(block, "ctx", 0, 0, tiled=True)
        back = back.reshape(n_ctx, heads, mine, block.shape[2])
        back = back.transpose(1, 0, 2, 3).reshape(heads, slots, block.shape[2])
        return jnp.einsum("hst,hsd->htd", place, back, preferred_element_type=jnp.float32).astype(
            jnp.bfloat16
        )

    def units(recv):
        width = recv.shape[2]
        block = recv.reshape(n_ctx, heads * per_dev, SEND_CAP, width).transpose(1, 0, 2, 3)
        return block.reshape(heads * per_dev, n_ctx * SEND_CAP, width)

    def ununits(block):
        width = block.shape[2]
        recv = block.reshape(heads * per_dev, n_ctx, SEND_CAP, width).transpose(1, 0, 2, 3)
        return recv.reshape(n_ctx, heads * mine, width)

    pos_slots = (
        jnp.sum(jnp.where(onehot, positions[None, None, :] + 1, 0), axis=2, dtype=jnp.int32) - 1
    )
    pos_slots = (
        pos_slots.reshape(heads, n_ctx, mine).transpose(1, 0, 2).reshape(n_ctx, heads * mine)
    )
    pos_recv = lax.all_to_all(pos_slots, "ctx", 0, 0, tiled=True)
    slot_pos = units(pos_recv[:, :, None])[:, :, 0]
    recv = to_owner(jnp.concatenate([queries, key_vectors, value_vectors], axis=2))
    block = units(recv)
    query_own, key_own, value_own = (
        block[:, :, :feature],
        block[:, :, feature : 2 * feature],
        block[:, :, 2 * feature :],
    )
    weights = weights_of(query_own, key_own, slot_pos, factor)
    rounded = weights.astype(jnp.bfloat16)
    out_own = jnp.einsum(
        "urj,ujd->urd", rounded, value_own, preferred_element_type=jnp.float32
    ).astype(jnp.bfloat16)
    attention = from_owner(ununits(out_own)).astype(jnp.float32)
    width_all = heads * feature * lax.axis_size("head")
    gain_full = norm_gain[:, None, :]
    scaled_grad = gain_full * upstream.astype(jnp.float32)
    sums = lax.psum(
        jnp.stack(
            [
                jnp.sum(attention * attention, axis=(0, 2)),
                jnp.sum(scaled_grad * attention, axis=(0, 2)),
            ]
        ),
        "head",
    )
    inverse = lax.rsqrt(sums[0] / width_all + 1e-06)[None, :, None]
    dot_total = sums[1][None, :, None]
    normed_out = (attention * inverse * gain_full).astype(jnp.bfloat16)
    grad_attention = (
        inverse * scaled_grad - attention * inverse * inverse * inverse * dot_total / width_all
    ).astype(jnp.bfloat16)
    grad_block = units(to_owner(grad_attention))
    delta_row = jnp.sum(grad_block.astype(jnp.float32) * out_own.astype(jnp.float32), axis=2)
    grad_value = jnp.einsum(
        "urj,urd->ujd", rounded, grad_block, preferred_element_type=jnp.float32
    ).astype(jnp.bfloat16)
    grad_prob = jnp.einsum(
        "urd,ujd->urj", grad_block, value_own, preferred_element_type=jnp.float32
    )
    grad_score = (factor * weights * (grad_prob - delta_row[:, :, None])).astype(jnp.bfloat16)
    grad_query = jnp.einsum(
        "urj,ujd->urd", grad_score, key_own, preferred_element_type=jnp.float32
    ).astype(jnp.bfloat16)
    grad_key = jnp.einsum(
        "urj,urd->ujd", grad_score, query_own, preferred_element_type=jnp.float32
    ).astype(jnp.bfloat16)
    grads = from_owner(ununits(jnp.concatenate([grad_query, grad_key, grad_value], axis=2)))
    cluster_sums = jnp.sum(key_own.astype(jnp.float32), axis=1)
    cluster_sums = cluster_sums.reshape(heads, per_dev, feature).transpose(1, 0, 2)
    centroids = cluster_sums * lax.rsqrt(
        jnp.mean(cluster_sums * cluster_sums, axis=2, keepdims=True) + 1e-06
    )
    return (
        normed_out,
        grads[:, :, :feature],
        grads[:, :, feature : 2 * feature],
        grads[:, :, 2 * feature :],
        centroids,
    )


def solution(mesh):
    tok = P("head", "ctx", None)
    in_specs = (tok, tok, tok, P("head", None), tok, tok, P("ctx"))
    out_specs = (tok, tok, tok, tok, P("ctx", "head", None))
    return jax.shard_map(local, mesh=mesh, in_specs=in_specs, out_specs=out_specs, check_vma=False)
```

profile of v0, /device:TPU:1, one launch (start us, length us, event | category | flops | bytes accessed | tf_op | source)
XLA Modules:
  0.0 322.7 jit_solution(3992617199061359926)
XLA Ops:
  4.6 20.4 %all-to-all-start = ((s32[128,1,16]{2,1,0:T(1,128)}), s32[128,1,16]{2,1,0:T(1,128)S(1)}, u32[]{:S(2)}, u32[]{:S(2)}) async-start(s32[128,1,16]{2,1,0:T(1,128)} %copy.97), calls=%async_computation | async-start | bytes 131072 | tf_op jit(solution)/shard_map/all_to_all | solution.py:77
  25.0 2.1 fusion.5
  27.8 2.1 copy.105
  29.8 10.1 %all-to-all-done = s32[128,1,16]{2,1,0:T(1,128)S(1)} async-done(((s32[128,1,16]{2,1,0:T(1,128)}), s32[128,1,16]{2,1,0:T(1,128)S(1)}, u32[]{:S(2)}, u32[]{:S(2)}) %all-to-all-start) | async-done | bytes 8224 | tf_op jit(solution)/shard_map/all_to_all | solution.py:77
  39.9 6.6 %all-to-all-start.1 = ((bf16[128,16,384]{2,1,0:T(8,128)(2,1)}), bf16[128,16,384]{2,1,0:T(8,128)(2,1)S(1)}, u32[]{:S(2)}, u32[]{:S(2)}) async-start(bf16[128,16,384]{2,1,0:T(8,128)(2,1)} %copy.105), calls=%async_computation.1 | async-start | bytes 3145728 | tf_op jit(solution)/shard_map/all_to_all | solution.py:51
  46.9 76.5 %all-to-all-done.1 = bf16[128,16,384]{2,1,0:T(8,128)(2,1)S(1)} async-done(((bf16[128,16,384]{2,1,0:T(8,128)(2,1)}), bf16[128,16,384]{2,1,0:T(8,128)(2,1)S(1)}, u32[]{:S(2)}, u32[]{:S(2)}) %all-to-all-start.1) | async-done | bytes 1572896 | tf_op jit(solution)/shard_map/all_to_all | solution.py:51
  123.8 1.6 copy.107
  126.1 2.8 fusion.49
  128.9 2.1 convolution_convert_fusion.4
  131.1 1.2 copy.110
  132.3 8.7 %all-to-all-start.2 = ((bf16[128,16,128]{2,1,0:T(8,128)(2,1)}), bf16[128,16,128]{2,1,0:T(8,128)(2,1)S(1)}, u32[]{:S(2)}, u32[]{:S(2)}) async-start(bf16[128,16,128]{2,1,0:T(8,128)(2,1)} %copy.110), calls=%async_computation.2 | async-start | bytes 1048576 | tf_op jit(solution)/shard_map/all_to_all | solution.py:54
  141.2 33.0 %all-to-all-done.2 = bf16[128,16,128]{2,1,0:T(8,128)(2,1)S(1)} async-done(((bf16[128,16,128]{2,1,0:T(8,128)(2,1)}), bf16[128,16,128]{2,1,0:T(8,128)(2,1)S(1)}, u32[]{:S(2)}, u32[]{:S(2)}) %all-to-all-start.2) | async-done | bytes 524320 | tf_op jit(solution)/shard_map/all_to_all | solution.py:54
  174.8 1.0 multiply_reduce_fusion.2
  175.8 8.7 %psum.7 = f32[2,256]{1,0:T(2,128)S(1)} all-reduce(f32[2,256]{1,0:T(2,128)S(1)} %pad_maximum_fusion.1), channel_id=1, replica_groups=mesh['ctx'=128,'head'=4] {'head'}, use_global_device_ids=true, to_apply=%region_6.7 | all-reduce | flops 512 | bytes 4096 | tf_op jit(solution)/shard_map/psum | solution.py:95
  184.5 0.8 convolution_convert_fusion
  185.8 42.3 %all_to_all.29 = bf16[128,16,128]{2,1,0:T(8,128)(2,1)S(1)} all-to-all(bf16[128,16,128]{2,1,0:T(8,128)(2,1)S(1)} %copy.119), channel_id=1, replica_groups=mesh['ctx'=128,'head'=4] {'ctx'}, dimensions={0} | all-to-all | bytes 1048576 | tf_op jit(solution)/shard_map/all_to_all | solution.py:51
  231.2 1.3 copy.129
  232.9 2.1 copy.131
  235.0 7.3 %all-to-all-start.4 = ((bf16[128,16,384]{2,1,0:T(8,128)(2,1)}), bf16[128,16,384]{2,1,0:T(8,128)(2,1)S(1)}, u32[]{:S(2)}, u32[]{:S(2)}) async-start(bf16[128,16,384]{2,1,0:T(8,128)(2,1)} %copy.131), calls=%async_computation.4 | async-start | bytes 3145728 | tf_op jit(solution)/shard_map/all_to_all | solution.py:54
  242.3 1.1 convert_reduce_fusion
  244.3 0.8 copy.134
  245.1 73.9 %all-to-all-done.4 = bf16[128,16,384]{2,1,0:T(8,128)(2,1)S(1)} async-done(((bf16[128,16,384]{2,1,0:T(8,128)(2,1)}), bf16[128,16,384]{2,1,0:T(8,128)(2,1)S(1)}, u32[]{:S(2)}, u32[]{:S(2)}) %all-to-all-start.4) | async-done | bytes 1572896 | tf_op jit(solution)/shard_map/all_to_all | solution.py:54
  319.4 1.2 copy.133
  321.8 0.9 fusion.47
  (56 shorter events, 13.0 us)
Async XLA Ops:
  4.6 35.4 %all-to-all-start = ((s32[128,1,16]{2,1,0:T(1,128)}), s32[128,1,16]{2,1,0:T(1,128)S(1)}, u32[]{:S(2)}, u32[]{:S(2)}) async-start(s32[128,1,16]{2,1,0:T(1,128)} %copy.97), calls=%async_computation | async-start | bytes 131072 | tf_op jit(solution)/shard_map/all_to_all | solution.py:77
  39.9 83.5 %all-to-all-start.1 = ((bf16[128,16,384]{2,1,0:T(8,128)(2,1)}), bf16[128,16,384]{2,1,0:T(8,128)(2,1)S(1)}, u32[]{:S(2)}, u32[]{:S(2)}) async-start(bf16[128,16,384]{2,1,0:T(8,128)(2,1)} %copy.105), calls=%async_computation.1 | async-start | bytes 3145728 | tf_op jit(solution)/shard_map/all_to_all | solution.py:51
  126.1 104.6 %copy-start = (bf16[8,256,384]{2,1,0:T(8,128)(2,1)}, bf16[8,256,384]{2,1,0:T(8,128)(2,1)S(1)}, u32[]{:S(2)}) copy-start(bf16[8,256,384]{2,1,0:T(8,128)(2,1)S(1)} %reshape.125) | copy-start | bytes 4718596
  131.0 10.0 %copy-start.3 = (bf16[4,256,128]{2,1,0:T(8,128)(2,1)S(1)}, bf16[4,256,128]{2,1,0:T(8,128)(2,1)}, u32[]{:S(2)}) copy-start(bf16[4,256,128]{2,1,0:T(8,128)(2,1)} %param.11) | copy-start | bytes 786436
  132.3 42.5 %copy-start.4 = (f32[4,128]{1,0:T(4,128)S(1)}, f32[4,128]{1,0:T(4,128)}, u32[]{:S(2)}) copy-start(f32[4,128]{1,0:T(4,128)} %param.10) | copy-start | bytes 6148
  132.3 41.9 %all-to-all-start.2 = ((bf16[128,16,128]{2,1,0:T(8,128)(2,1)}), bf16[128,16,128]{2,1,0:T(8,128)(2,1)S(1)}, u32[]{:S(2)}, u32[]{:S(2)}) async-start(bf16[128,16,128]{2,1,0:T(8,128)(2,1)} %copy.110), calls=%async_computation.2 | async-start | bytes 1048576 | tf_op jit(solution)/shard_map/all_to_all | solution.py:54
  175.7 9.6 %copy-start.1 = (f32[4,256,128]{1,2,0:T(8,128)}, f32[4,256,128]{1,2,0:T(8,128)S(1)}, u32[]{:S(2)}) copy-start(f32[4,256,128]{1,2,0:T(8,128)S(1)} %get-tuple-element.34) | copy-start | bytes 1572868
  185.4 43.4 %copy-start.5 = (f32[8,256,256]{1,2,0:T(8,128)S(1)}, f32[8,256,256]{1,2,0:T(8,128)}, u32[]{:S(2)}) copy-start(f32[8,256,256]{1,2,0:T(8,128)} %get-tuple-element.33) | copy-start | bytes 6291460
  235.0 9.2 %copy-start.2 = (f32[4,256,128]{1,2,0:T(8,128)S(1)}, f32[4,256,128]{1,2,0:T(8,128)}, u32[]{:S(2)}) copy-start(f32[4,256,128]{1,2,0:T(8,128)} %copy-done.1) | copy-start | bytes 1572868
  235.0 84.1 %all-to-all-start.4 = ((bf16[128,16,384]{2,1,0:T(8,128)(2,1)}), bf16[128,16,384]{2,1,0:T(8,128)(2,1)S(1)}, u32[]{:S(2)}, u32[]{:S(2)}) async-start(bf16[128,16,384]{2,1,0:T(8,128)(2,1)} %copy.131), calls=%async_computation.4 | async-start | bytes 3145728 | tf_op jit(solution)/shard_map/all_to_all | solution.py:54
where the time goes:
time: 323 us
  waiting for transfers between devices  194 us (60%)
  blocking collectives  51 us (16%)
  starting transfers between devices  43 us (13%)
  local copies, waits for them, and re-layouts  18.7 us (6%)
  matrix products  11.4 us (4%)
  other arithmetic  4.03 us (1%)
    all_to_all x2, waiting for transfers between devices, from_owner(): back = lax.all_to_all(block, 'ctx', 0, 0, tiled=True)  107 us
    all_to_all x1, waiting for transfers between devices, to_owner(): return lax.all_to_all(placed, 'ctx', 0, 0, tiled=True)  76.5 us
    all_to_all x1, blocking collectives, to_owner(): return lax.all_to_all(placed, 'ctx', 0, 0, tiled=True)  42.3 us
    all_to_all x1, starting transfers between devices, local(): pos_recv = lax.all_to_all(pos_slots, 'ctx', 0, 0, tiled=True)  20.4 us
    all_to_all x2, starting transfers between devices, from_owner(): back = lax.all_to_all(block, 'ctx', 0, 0, tiled=True)  16 us
    all_to_all x1, waiting for transfers between devices, local(): pos_recv = lax.all_to_all(pos_slots, 'ctx', 0, 0, tiled=True)  10.1 us
    psum x1, blocking collectives, local(): lax.psum(jnp.stack([jnp.sum(attention * attention, axis=(0, 2)), jnp.sum(...  8.73 us
    all_to_all x1, starting transfers between devices, to_owner(): return lax.all_to_all(placed, 'ctx', 0, 0, tiled=True)  6.58 us
  transfers between devices with their start and end apart: 4, of which 4 were waited for; matrix products, arithmetic and copies ran while one was open for 3% of the time, Pallas kernels for 0%

commit v1 on v0

--- a/solution.py
+++ b/solution.py
@@ -92,15 +92,11 @@
     width_all = heads * feature * lax.axis_size("head")
     gain_full = norm_gain[:, None, :]
     scaled_grad = gain_full * upstream.astype(jnp.float32)
-    sums = lax.psum(
-        jnp.stack(
-            [
-                jnp.sum(attention * attention, axis=(0, 2)),
-                jnp.sum(scaled_grad * attention, axis=(0, 2)),
-            ]
-        ),
-        "head",
+    x = jnp.stack(
+        [jnp.sum(attention * attention, axis=(0, 2)), jnp.sum(scaled_grad * attention, axis=(0, 2))]
     )
+    blocks = lax.all_gather(x, "head")
+    sums = jnp.sum(blocks, axis=0)
     inverse = lax.rsqrt(sums[0] / width_all + 1e-06)[None, :, None]
     dot_total = sums[1][None, :, None]
     normed_out = (attention * inverse * gain_full).astype(jnp.bfloat16)

time: 323 us -> 324 us (level)
    psum x1 -> x0, blocking collectives: 8.73 us -> none  [local(): lax.psum(jnp.stack([jnp.sum(attention * attention, axis=(0, 2)), jnp.sum(...]
    all_gather x0 -> x1, blocking collectives: none -> 8.6 us  [local(): blocks = lax.all_gather(x, 'head')]
where the time goes in v1:
time: 324 us; the launch traced here: 323 us
  waiting for transfers between devices  194 us (60%)
  blocking collectives  51.5 us (16%)
  starting transfers between devices  43 us (13%)
  local copies, waits for them, and re-layouts  18.7 us (6%)
  matrix products  11.4 us (4%)
  other arithmetic  4.04 us (1%)
    all_to_all x2, waiting for transfers between devices, from_owner(): back = lax.all_to_all(block, 'ctx', 0, 0, tiled=True)  107 us
    all_to_all x1, waiting for transfers between devices, to_owner(): return lax.all_to_all(placed, 'ctx', 0, 0, tiled=True)  76.5 us
    all_to_all x1, blocking collectives, to_owner(): return lax.all_to_all(placed, 'ctx', 0, 0, tiled=True)  42.9 us
    all_to_all x1, starting transfers between devices, local(): pos_recv = lax.all_to_all(pos_slots, 'ctx', 0, 0, tiled=True)  20.4 us
    all_to_all x2, starting transfers between devices, from_owner(): back = lax.all_to_all(block, 'ctx', 0, 0, tiled=True)  16 us
    all_to_all x1, waiting for transfers between devices, local(): pos_recv = lax.all_to_all(pos_slots, 'ctx', 0, 0, tiled=True)  10.1 us
    all_gather x1, blocking collectives, local(): blocks = lax.all_gather(x, 'head')  8.6 us
    all_to_all x1, starting transfers between devices, to_owner(): return lax.all_to_all(placed, 'ctx', 0, 0, tiled=True)  6.58 us
  transfers between devices with their start and end apart: 4, of which 4 were waited for; matrix products, arithmetic and copies ran while one was open for 3% of the time, Pallas kernels for 0%

profile of v1, /device:TPU:1, one launch (start us, length us, event | category | flops | bytes accessed | tf_op | source)
XLA Modules:
  0.0 323.3 jit_solution(7042655276126263743)
XLA Ops:
  4.6 20.4 %all-to-all-start = ((s32[128,1,16]{2,1,0:T(1,128)}), s32[128,1,16]{2,1,0:T(1,128)S(1)}, u32[]{:S(2)}, u32[]{:S(2)}) async-start(s32[128,1,16]{2,1,0:T(1,128)} %copy.97), calls=%async_computation | async-start | bytes 131072 | tf_op jit(solution)/shard_map/all_to_all | solution.py:77
  25.0 2.1 fusion.5
  27.8 2.1 copy.105
  29.8 10.1 %all-to-all-done = s32[128,1,16]{2,1,0:T(1,128)S(1)} async-done(((s32[128,1,16]{2,1,0:T(1,128)}), s32[128,1,16]{2,1,0:T(1,128)S(1)}, u32[]{:S(2)}, u32[]{:S(2)}) %all-to-all-start) | async-done | bytes 8224 | tf_op jit(solution)/shard_map/all_to_all | solution.py:77
  39.9 6.6 %all-to-all-start.1 = ((bf16[128,16,384]{2,1,0:T(8,128)(2,1)}), bf16[128,16,384]{2,1,0:T(8,128)(2,1)S(1)}, u32[]{:S(2)}, u32[]{:S(2)}) async-start(bf16[128,16,384]{2,1,0:T(8,128)(2,1)} %copy.105), calls=%async_computation.1 | async-start | bytes 3145728 | tf_op jit(solution)/shard_map/all_to_all | solution.py:51
  46.9 76.5 %all-to-all-done.1 = bf16[128,16,384]{2,1,0:T(8,128)(2,1)S(1)} async-done(((bf16[128,16,384]{2,1,0:T(8,128)(2,1)}), bf16[128,16,384]{2,1,0:T(8,128)(2,1)S(1)}, u32[]{:S(2)}, u32[]{:S(2)}) %all-to-all-start.1) | async-done | bytes 1572896 | tf_op jit(solution)/shard_map/all_to_all | solution.py:51
  123.8 1.6 copy.107
  126.1 2.8 fusion.49
  128.9 2.1 convolution_convert_fusion.4
  131.1 1.2 copy.110
  132.3 8.7 %all-to-all-start.2 = ((bf16[128,16,128]{2,1,0:T(8,128)(2,1)}), bf16[128,16,128]{2,1,0:T(8,128)(2,1)S(1)}, u32[]{:S(2)}, u32[]{:S(2)}) async-start(bf16[128,16,128]{2,1,0:T(8,128)(2,1)} %copy.110), calls=%async_computation.2 | async-start | bytes 1048576 | tf_op jit(solution)/shard_map/all_to_all | solution.py:54
  141.2 33.0 %all-to-all-done.2 = bf16[128,16,128]{2,1,0:T(8,128)(2,1)S(1)} async-done(((bf16[128,16,128]{2,1,0:T(8,128)(2,1)}), bf16[128,16,128]{2,1,0:T(8,128)(2,1)S(1)}, u32[]{:S(2)}, u32[]{:S(2)}) %all-to-all-start.2) | async-done | bytes 524320 | tf_op jit(solution)/shard_map/all_to_all | solution.py:54
  174.8 1.0 multiply_reduce_fusion.2
  175.8 8.6 %all-gather.1 = f32[4,2,256]{2,1,0:T(2,128)S(1)} all-gather(f32[1,2,256]{2,1,0:T(2,128)S(1)} %maximum_bitcast_fusion), channel_id=2, replica_groups=mesh['ctx'=128,'head'=4] {'head'}, dimensions={0}, use_global_device_ids=true | all-gather | bytes 10240 | tf_op jit(solution)/shard_map/all_gather | solution.py:98
  184.4 0.8 convolution_convert_fusion
  185.7 42.9 %all_to_all.29 = bf16[128,16,128]{2,1,0:T(8,128)(2,1)S(1)} all-to-all(bf16[128,16,128]{2,1,0:T(8,128)(2,1)S(1)} %copy.119), channel_id=1, replica_groups=mesh['ctx'=128,'head'=4] {'ctx'}, dimensions={0} | all-to-all | bytes 1048576 | tf_op jit(solution)/shard_map/all_to_all | solution.py:51
  231.7 1.3 copy.129
  233.4 2.1 copy.131
  235.5 7.3 %all-to-all-start.4 = ((bf16[128,16,384]{2,1,0:T(8,128)(2,1)}), bf16[128,16,384]{2,1,0:T(8,128)(2,1)S(1)}, u32[]{:S(2)}, u32[]{:S(2)}) async-start(bf16[128,16,384]{2,1,0:T(8,128)(2,1)} %copy.131), calls=%async_computation.4 | async-start | bytes 3145728 | tf_op jit(solution)/shard_map/all_to_all | solution.py:54
  242.8 1.1 convert_reduce_fusion
  244.8 0.8 copy.134
  245.7 73.9 %all-to-all-done.4 = bf16[128,16,384]{2,1,0:T(8,128)(2,1)S(1)} async-done(((bf16[128,16,384]{2,1,0:T(8,128)(2,1)}), bf16[128,16,384]{2,1,0:T(8,128)(2,1)S(1)}, u32[]{:S(2)}, u32[]{:S(2)}) %all-to-all-start.4) | async-done | bytes 1572896 | tf_op jit(solution)/shard_map/all_to_all | solution.py:54
  319.9 1.2 copy.133
  322.3 0.9 fusion.47
  (57 shorter events, 13.0 us)
Async XLA Ops:
  4.6 35.4 %all-to-all-start = ((s32[128,1,16]{2,1,0:T(1,128)}), s32[128,1,16]{2,1,0:T(1,128)S(1)}, u32[]{:S(2)}, u32[]{:S(2)}) async-start(s32[128,1,16]{2,1,0:T(1,128)} %copy.97), calls=%async_computation | async-start | bytes 131072 | tf_op jit(solution)/shard_map/all_to_all | solution.py:77
  39.9 83.5 %all-to-all-start.1 = ((bf16[128,16,384]{2,1,0:T(8,128)(2,1)}), bf16[128,16,384]{2,1,0:T(8,128)(2,1)S(1)}, u32[]{:S(2)}, u32[]{:S(2)}) async-start(bf16[128,16,384]{2,1,0:T(8,128)(2,1)} %copy.105), calls=%async_computation.1 | async-start | bytes 3145728 | tf_op jit(solution)/shard_map/all_to_all | solution.py:51
  126.1 105.1 %copy-start = (bf16[8,256,384]{2,1,0:T(8,128)(2,1)}, bf16[8,256,384]{2,1,0:T(8,128)(2,1)S(1)}, u32[]{:S(2)}) copy-start(bf16[8,256,384]{2,1,0:T(8,128)(2,1)S(1)} %reshape.125) | copy-start | bytes 4718596
  131.0 10.0 %copy-start.3 = (bf16[4,256,128]{2,1,0:T(8,128)(2,1)S(1)}, bf16[4,256,128]{2,1,0:T(8,128)(2,1)}, u32[]{:S(2)}) copy-start(bf16[4,256,128]{2,1,0:T(8,128)(2,1)} %param.11) | copy-start | bytes 786436
  132.3 42.5 %copy-start.4 = (f32[4,128]{1,0:T(4,128)S(1)}, f32[4,128]{1,0:T(4,128)}, u32[]{:S(2)}) copy-start(f32[4,128]{1,0:T(4,128)} %param.10) | copy-start | bytes 6148
  132.3 41.9 %all-to-all-start.2 = ((bf16[128,16,128]{2,1,0:T(8,128)(2,1)}), bf16[128,16,128]{2,1,0:T(8,128)(2,1)S(1)}, u32[]{:S(2)}, u32[]{:S(2)}) async-start(bf16[128,16,128]{2,1,0:T(8,128)(2,1)} %copy.110), calls=%async_computation.2 | async-start | bytes 1048576 | tf_op jit(solution)/shard_map/all_to_all | solution.py:54
  175.7 9.5 %copy-start.1 = (f32[4,256,128]{1,2,0:T(8,128)}, f32[4,256,128]{1,2,0:T(8,128)S(1)}, u32[]{:S(2)}) copy-start(f32[4,256,128]{1,2,0:T(8,128)S(1)} %get-tuple-element.34) | copy-start | bytes 1572868
  185.3 44.0 %copy-start.5 = (f32[8,256,256]{1,2,0:T(8,128)S(1)}, f32[8,256,256]{1,2,0:T(8,128)}, u32[]{:S(2)}) copy-start(f32[8,256,256]{1,2,0:T(8,128)} %get-tuple-element.33) | copy-start | bytes 6291460
  235.5 9.2 %copy-start.2 = (f32[4,256,128]{1,2,0:T(8,128)S(1)}, f32[4,256,128]{1,2,0:T(8,128)}, u32[]{:S(2)}) copy-start(f32[4,256,128]{1,2,0:T(8,128)} %copy-done.1) | copy-start | bytes 1572868
  235.5 84.1 %all-to-all-start.4 = ((bf16[128,16,384]{2,1,0:T(8,128)(2,1)}), bf16[128,16,384]{2,1,0:T(8,128)(2,1)S(1)}, u32[]{:S(2)}, u32[]{:S(2)}) async-start(bf16[128,16,384]{2,1,0:T(8,128)(2,1)} %copy.131), calls=%async_computation.4 | async-start | bytes 3145728 | tf_op jit(solution)/shard_map/all_to_all | solution.py:54
